TPU v7x, 32 devices: a whole 2x2x4 slice. The times are simulated.
32 devices in a mesh: surf: 4 (over y, x), norm: 8 (over z, core).
Axes of the slice: x: 2, y: 2, z: 4, core: 2. Of those that a mesh axis runs over, the one named last changes fastest.
Arguments:
- rhs: float32 [32, 48, 512], P('norm', None, 'surf'), may hold values from -6 to 6
- previous: float32 [32, 48, 512], P('norm', None, 'surf'), may hold values from -6 to 6
- minus_jac: bfloat16 [32, 48, 48, 512], P('norm', None, None, 'surf'), may hold values from -0.4375 to 0.4375
- plus_jac: bfloat16 [32, 48, 48, 512], P('norm', None, None, 'surf'), may hold values from -0.4375 to 0.4375
- dissipation: float32 [32, 48, 512], P('norm', None, 'surf'), may hold values from 0.01 to 0.08
- inverse_diag: bfloat16 [32, 48, 48, 512], P('norm', None, None, 'surf'), may hold values from -0.15625 to 0.15625
- lower_coupling: bfloat16 [32, 48, 48, 512], P('norm', None, None, 'surf'), may hold values from -0.1484375 to 1, as said below
- upper_coupling: bfloat16 [32, 48, 48, 512], P('norm', None, None, 'surf'), may hold values from -0.1484375 to 1, as said below
Outputs:
- update: float32 [32, 48, 512], P('norm', None, 'surf')
Inputs may be any that keep to these rules, and one draw needn't show every extreme that they name: `lower_coupling`: diagonal entries in (0, 1], off-diagonal entries small. `upper_coupling`: diagonal entries in (0, 1], off-diagonal entries small.
All inputs are finite; a program needn't handle non-finite values.
Results may differ from a plain program's by a relative error of at most 0.0003.
Values may be sent and summed in bfloat16 or wider, within the bound.
A program may use at most 512 MiB of HBM per device.

v0:
```python
import jax
import jax.numpy as jnp
from jax import lax
from jax.sharding import PartitionSpec as P

SWEEPS = 2


HIGH = lax.Precision.HIGHEST


def with_halo(cells, sides, width):
    for axis, dim in sides:
        count = lax.axis_size(axis)
        ends = count - 1
        head = lax.slice_in_dim(cells, 0, width, axis=dim)
        tail = lax.slice_in_dim(cells, cells.shape[dim] - width, cells.shape[dim], axis=dim)
        cells = jnp.concatenate(
            [
                lax.ppermute(tail, axis, [(i, (i + 1) % count) for i in range(ends)]),
                cells,
                lax.ppermute(head, axis, [((i + 1) % count, i) for i in range(ends)]),
            ],
            axis=dim,
        )
    return cells


def passed_along(value, axis, by):
    length = lax.axis_size(axis)
    pairs = [(i, i + by) for i in range(length) if 0 <= i + by < length]
    return lax.ppermute(value, axis, pairs)


def matvec(block, vector):
    return jnp.einsum("abs,bs->as", block.astype(jnp.float32), vector, precision=HIGH)


def advance(carry, items):
    source_cell, block = items
    value = source_cell + matvec(block, carry)
    return (value, value)


def run_forward(source, cell_block_set, start):
    return lax.scan(advance, start, (source, cell_block_set))[1]


def run_backward(values, cell_block_set, start):
    return lax.scan(advance, start, (values, cell_block_set), reverse=True)[1]


def shards(
    rhs, previous, minus_jac, plus_jac, dissipation, inverse_diag, lower_coupling, upper_coupling
):
    equations = rhs.shape[1]
    width = rhs.shape[2]
    zeros_line = jnp.zeros((equations, width), jnp.float32)
    delta = previous
    for sweep_index in range(SWEEPS):
        padded = with_halo(delta, (("surf", 2),), 2)
        left_two = padded[:, :, 0:width]
        left_one = padded[:, :, 1 : width + 1]
        centre = padded[:, :, 2 : width + 2]
        right_one = padded[:, :, 3 : width + 3]
        right_two = padded[:, :, 4 : width + 4]
        fourth = left_two - 4.0 * left_one + 6.0 * centre - 4.0 * right_one + right_two

        def per_cell(items):
            residual_cell, below, above, minus_block, plus_block, inverse_block = items
            return matvec(
                inverse_block,
                residual_cell - matvec(minus_block, below) - matvec(plus_block, above),
            )

        source = lax.map(
            per_cell,
            (rhs - dissipation * fourth, left_one, right_one, minus_jac, plus_jac, inverse_diag),
        )
        incoming = zeros_line
        for relay_round in range(lax.axis_size("norm") - 1):
            partial_run = run_forward(source, lower_coupling, incoming)
            incoming = passed_along(partial_run[-1], "norm", 1)
        forward_values = run_forward(source, lower_coupling, incoming)
        incoming = zeros_line
        for relay_round in range(lax.axis_size("norm") - 1):
            partial_run = run_backward(forward_values, upper_coupling, incoming)
            incoming = passed_along(partial_run[0], "norm", -1)
        delta = run_backward(forward_values, upper_coupling, incoming)
    return delta


def solution(mesh):
    return jax.shard_map(
        shards,
        mesh=mesh,
        in_specs=(
            P("norm", None, "surf"),
            P("norm", None, "surf"),
            P("norm", None, None, "surf"),
            P("norm", None, None, "surf"),
            P("norm", None, "surf"),
            P("norm", None, None, "surf"),
            P("norm", None, None, "surf"),
            P("norm", None, None, "surf"),
        ),
        out_specs=P("norm", None, "surf"),
        check_vma=False,
    )
```

profile of v0, /device:TPU:5, one launch (start us, length us, event | category | flops | bytes accessed | tf_op | source)
XLA Modules:
  0.0 286.1 jit_solution(13893202865682685663)
XLA Ops:
  11.8 12.0 %while.472 = (s32[]{:T(128)}, f32[4,48,128]{2,1,0:T(8,128)S(1)}, f32[4,48,128]{2,1,0:T(8,128)S(1)}, f32[4,48,128]{2,1,0:T(8,128)S(1)}, bf16[4,48,48,128]{3,2,1,0...) while((s32[]{:T(128)}, f32[4,48,128]{2,1,0:T(8,128)S(1)}, ...), condition=%wide.region_1.2_spmd, body=%wide.region_0.1_spmd.sunk | while | flops 2648066 | bytes 2162805 | solution.py:76
  24.7 5.2 %collective-permute-start.2 = (f32[48,128]{1,0:T(8,128)S(1)}, f32[48,128]{1,0:T(8,128)S(1)}, u32[]{:S(2)}, u32[]{:S(2)}) collective-permute-start(f32[48,128]{1,0:T(8,128)S(1)} %slice_bitcast_fusion.27), channel_id=1, source_target_pairs={{0,1},{1,2},{2,3},{3,4},{4,5},{5,6},{6,7},{8,9},{9,10},{10,11},{11... | collective-permute-start | bytes 73736 | tf_op jit(solution)/shard_map/ppermute | solution.py:32
  37.7 4.2 %collective-permute-start.4 = (f32[48,128]{1,0:T(8,128)S(1)}, f32[48,128]{1,0:T(8,128)S(1)}, u32[]{:S(2)}, u32[]{:S(2)}) collective-permute-start(f32[48,128]{1,0:T(8,128)S(1)} %slice_bitcast_fusion.25), channel_id=1, source_target_pairs={{0,1},{1,2},{2,3},{3,4},{4,5},{5,6},{6,7},{8,9},{9,10},{10,11},{11... | collective-permute-start | bytes 73736 | tf_op jit(solution)/shard_map/ppermute | solution.py:32
  43.7 4.2 %collective-permute-start.5 = (f32[48,128]{1,0:T(8,128)S(1)}, f32[48,128]{1,0:T(8,128)S(1)}, u32[]{:S(2)}, u32[]{:S(2)}) collective-permute-start(f32[48,128]{1,0:T(8,128)S(1)} %slice_bitcast_fusion.24), channel_id=1, source_target_pairs={{0,1},{1,2},{2,3},{3,4},{4,5},{5,6},{6,7},{8,9},{9,10},{10,11},{11... | collective-permute-start | bytes 73736 | tf_op jit(solution)/shard_map/ppermute | solution.py:32
  49.7 4.2 %collective-permute-start.6 = (f32[48,128]{1,0:T(8,128)S(1)}, f32[48,128]{1,0:T(8,128)S(1)}, u32[]{:S(2)}, u32[]{:S(2)}) collective-permute-start(f32[48,128]{1,0:T(8,128)S(1)} %slice_bitcast_fusion.23), channel_id=1, source_target_pairs={{0,1},{1,2},{2,3},{3,4},{4,5},{5,6},{6,7},{8,9},{9,10},{10,11},{11... | collective-permute-start | bytes 73736 | tf_op jit(solution)/shard_map/ppermute | solution.py:32
  67.7 5.1 %while.503 = (s32[]{:T(128)}, f32[48,128]{1,0:T(8,128)S(1)}, f32[4,48,128]{2,1,0:T(8,128)S(1)}, f32[4,48,128]{2,1,0:T(8,128)S(1)}, bf16[4,48,48,128]{3,2,1,0:T(8,128)(2,1)}, /*index=5*/s32[]{:T(128)}, s32[]{:T(128)}, s32[]{:T(128)}) while((s32[]{:T(128)}, f32[48,128]{1,0:T(8,128)S(1)}, f32[4,48,128]{2,1,0:T(8,128)S(1)}, ...), condition=%wide.region_19.20_spmd.clone, body=%wide.region_18.19_spmd.clone.sunk | while | flops 890884 | bytes 786547 | solution.py:50
  78.7 5.1 %while.480 = (s32[]{:T(128)}, f32[48,128]{1,0:T(8,128)S(1)}, f32[4,48,128]{2,1,0:T(8,128)S(1)}, f32[4,48,128]{2,1,0:T(8,128)S(1)}, bf16[4,48,48,128]{3,2,1,0:T(8,128)(2,1)}, /*index=5*/s32[]{:T(128)}, s32[]{:T(128)}) while((s32[]{:T(128)}, f32[48,128]{1,0:T(8,128)S(1)}, f32[4,48,128]{2,1,0:T(8,128)S(1)}, f32[4,48,128]{2,1,0:T(8,128)S(1)}, ...), condition=%wide.region_21.22_spmd, body=%wide.region_20.21_spmd.sunk | while | flops 884739 | bytes 737377 | solution.py:50
  88.9 5.1 %while.481 = (s32[]{:T(128)}, f32[48,128]{1,0:T(8,128)S(1)}, f32[4,48,128]{2,1,0:T(8,128)S(1)}, f32[4,48,128]{2,1,0:T(8,128)S(1)}, bf16[4,48,48,128]{3,2,1,0:T(8,128)(2,1)}, /*index=5*/s32[]{:T(128)}, s32[]{:T(128)}) while((s32[]{:T(128)}, f32[48,128]{1,0:T(8,128)S(1)}, f32[4,48,128]{2,1,0:T(8,128)S(1)}, f32[4,48,128]{2,1,0:T(8,128)S(1)}, ...), condition=%wide.region_23.24_spmd, body=%wide.region_22.23_spmd.sunk | while | flops 884739 | bytes 737377 | solution.py:50
  99.1 5.1 %while.482 = (s32[]{:T(128)}, f32[48,128]{1,0:T(8,128)S(1)}, f32[4,48,128]{2,1,0:T(8,128)S(1)}, f32[4,48,128]{2,1,0:T(8,128)S(1)}, bf16[4,48,48,128]{3,2,1,0:T(8,128)(2,1)}, /*index=5*/s32[]{:T(128)}, s32[]{:T(128)}) while((s32[]{:T(128)}, f32[48,128]{1,0:T(8,128)S(1)}, f32[4,48,128]{2,1,0:T(8,128)S(1)}, f32[4,48,128]{2,1,0:T(8,128)S(1)}, ...), condition=%wide.region_25.26_spmd, body=%wide.region_24.25_spmd.sunk | while | flops 884739 | bytes 737377 | solution.py:50
  109.4 5.1 %while.483 = (s32[]{:T(128)}, f32[48,128]{1,0:T(8,128)S(1)}, f32[4,48,128]{2,1,0:T(8,128)S(1)}, f32[4,48,128]{2,1,0:T(8,128)S(1)}, bf16[4,48,48,128]{3,2,1,0:T(8,128)(2,1)}, /*index=5*/s32[]{:T(128)}, s32[]{:T(128)}) while((s32[]{:T(128)}, f32[48,128]{1,0:T(8,128)S(1)}, f32[4,48,128]{2,1,0:T(8,128)S(1)}, f32[4,48,128]{2,1,0:T(8,128)S(1)}, ...), condition=%wide.region_27.28_spmd, body=%wide.region_26.27_spmd.sunk | while | flops 884739 | bytes 737377 | solution.py:50
  119.6 5.1 %while.484 = (s32[]{:T(128)}, f32[48,128]{1,0:T(8,128)S(1)}, f32[4,48,128]{2,1,0:T(8,128)S(1)}, f32[4,48,128]{2,1,0:T(8,128)S(1)}, bf16[4,48,48,128]{3,2,1,0:T(8,128)(2,1)}, /*index=5*/s32[]{:T(128)}, s32[]{:T(128)}) while((s32[]{:T(128)}, f32[48,128]{1,0:T(8,128)S(1)}, f32[4,48,128]{2,1,0:T(8,128)S(1)}, f32[4,48,128]{2,1,0:T(8,128)S(1)}, ...), condition=%wide.region_29.30_spmd, body=%wide.region_28.29_spmd.sunk | while | flops 884739 | bytes 737377 | solution.py:50
  129.9 5.1 %while.485 = (s32[]{:T(128)}, f32[48,128]{1,0:T(8,128)S(1)}, f32[4,48,128]{2,1,0:T(8,128)S(1)}, f32[4,48,128]{2,1,0:T(8,128)S(1)}, bf16[4,48,48,128]{3,2,1,0:T(8,128)(2,1)}, /*index=5*/s32[]{:T(128)}, s32[]{:T(128)}) while((s32[]{:T(128)}, f32[48,128]{1,0:T(8,128)S(1)}, f32[4,48,128]{2,1,0:T(8,128)S(1)}, f32[4,48,128]{2,1,0:T(8,128)S(1)}, ...), condition=%wide.region_31.32_spmd, body=%wide.region_30.31_spmd.sunk | while | flops 884739 | bytes 737377 | solution.py:50
  140.1 5.1 %while.486 = (s32[]{:T(128)}, f32[48,128]{1,0:T(8,128)S(1)}, f32[4,48,128]{2,1,0:T(8,128)S(1)}, f32[4,48,128]{2,1,0:T(8,128)S(1)}, bf16[4,48,48,128]{3,2,1,0:T(8,128)(2,1)}, /*index=5*/s32[]{:T(128)}, s32[]{:T(128)}) while((s32[]{:T(128)}, f32[48,128]{1,0:T(8,128)S(1)}, f32[4,48,128]{2,1,0:T(8,128)S(1)}, f32[4,48,128]{2,1,0:T(8,128)S(1)}, ...), condition=%wide.region_33.34_spmd, body=%wide.region_32.33_spmd.sunk | while | flops 884739 | bytes 737377 | solution.py:50
  153.8 12.0 %while.487 = (s32[]{:T(128)}, f32[4,48,128]{2,1,0:T(8,128)S(1)}, f32[4,48,128]{2,1,0:T(8,128)S(1)}, f32[4,48,128]{2,1,0:T(8,128)S(1)}, bf16[4,48,48,128]{3,2,1,0...) while((s32[]{:T(128)}, f32[4,48,128]{2,1,0:T(8,128)S(1)}, ...), condition=%wide.region_35.36_spmd, body=%wide.region_34.35_spmd.sunk | while | flops 2648066 | bytes 2162805 | solution.py:76
  183.9 4.2 %collective-permute-start.21 = (f32[48,128]{1,0:T(8,128)S(1)}, f32[48,128]{1,0:T(8,128)S(1)}, u32[]{:S(2)}, u32[]{:S(2)}) collective-permute-start(f32[48,128]{1,0:T(8,128)S(1)} %slice_bitcast_fusion.10), channel_id=1, source_target_pairs={{0,1},{1,2},{2,3},{3,4},{4,5},{5,6},{6,7},{8,9},{9,10},{10,11},{11... | collective-permute-start | bytes 73736 | tf_op jit(solution)/shard_map/ppermute | solution.py:32
  189.9 4.2 %collective-permute-start.22 = (f32[48,128]{1,0:T(8,128)S(1)}, f32[48,128]{1,0:T(8,128)S(1)}, u32[]{:S(2)}, u32[]{:S(2)}) collective-permute-start(f32[48,128]{1,0:T(8,128)S(1)} %slice_bitcast_fusion.9), channel_id=1, source_target_pairs={{0,1},{1,2},{2,3},{3,4},{4,5},{5,6},{6,7},{8,9},{9,10},{10,11},{11... | collective-permute-start | bytes 73736 | tf_op jit(solution)/shard_map/ppermute | solution.py:32
  207.9 5.1 %while.505 = (s32[]{:T(128)}, f32[48,128]{1,0:T(8,128)S(1)}, f32[4,48,128]{2,1,0:T(8,128)S(1)}, f32[4,48,128]{2,1,0:T(8,128)S(1)}, bf16[4,48,48,128]{3,2,1,0:T(8,128)(2,1)}, /*index=5*/s32[]{:T(128)}, s32[]{:T(128)}, s32[]{:T(128)}) while((s32[]{:T(128)}, f32[48,128]{1,0:T(8,128)S(1)}, f32[4,48,128]{2,1,0:T(8,128)S(1)}, ...), condition=%wide.region_53.54_spmd.clone, body=%wide.region_52.53_spmd.clone.sunk | while | flops 890884 | bytes 786547 | solution.py:50
  218.8 5.1 %while.495 = (s32[]{:T(128)}, f32[48,128]{1,0:T(8,128)S(1)}, f32[4,48,128]{2,1,0:T(8,128)S(1)}, f32[4,48,128]{2,1,0:T(8,128)S(1)}, bf16[4,48,48,128]{3,2,1,0:T(8,128)(2,1)}, /*index=5*/s32[]{:T(128)}, s32[]{:T(128)}) while((s32[]{:T(128)}, f32[48,128]{1,0:T(8,128)S(1)}, f32[4,48,128]{2,1,0:T(8,128)S(1)}, f32[4,48,128]{2,1,0:T(8,128)S(1)}, ...), condition=%wide.region_55.56_spmd, body=%wide.region_54.55_spmd.sunk | while | flops 884739 | bytes 737377 | solution.py:50
  229.1 5.1 %while.496 = (s32[]{:T(128)}, f32[48,128]{1,0:T(8,128)S(1)}, f32[4,48,128]{2,1,0:T(8,128)S(1)}, f32[4,48,128]{2,1,0:T(8,128)S(1)}, bf16[4,48,48,128]{3,2,1,0:T(8,128)(2,1)}, /*index=5*/s32[]{:T(128)}, s32[]{:T(128)}) while((s32[]{:T(128)}, f32[48,128]{1,0:T(8,128)S(1)}, f32[4,48,128]{2,1,0:T(8,128)S(1)}, f32[4,48,128]{2,1,0:T(8,128)S(1)}, ...), condition=%wide.region_57.58_spmd, body=%wide.region_56.57_spmd.sunk | while | flops 884739 | bytes 737377 | solution.py:50
  239.4 5.1 %while.497 = (s32[]{:T(128)}, f32[48,128]{1,0:T(8,128)S(1)}, f32[4,48,128]{2,1,0:T(8,128)S(1)}, f32[4,48,128]{2,1,0:T(8,128)S(1)}, bf16[4,48,48,128]{3,2,1,0:T(8,128)(2,1)}, /*index=5*/s32[]{:T(128)}, s32[]{:T(128)}) while((s32[]{:T(128)}, f32[48,128]{1,0:T(8,128)S(1)}, f32[4,48,128]{2,1,0:T(8,128)S(1)}, f32[4,48,128]{2,1,0:T(8,128)S(1)}, ...), condition=%wide.region_59.60_spmd, body=%wide.region_58.59_spmd.sunk | while | flops 884739 | bytes 737377 | solution.py:50
  249.6 5.1 %while.498 = (s32[]{:T(128)}, f32[48,128]{1,0:T(8,128)S(1)}, f32[4,48,128]{2,1,0:T(8,128)S(1)}, f32[4,48,128]{2,1,0:T(8,128)S(1)}, bf16[4,48,48,128]{3,2,1,0:T(8,128)(2,1)}, /*index=5*/s32[]{:T(128)}, s32[]{:T(128)}) while((s32[]{:T(128)}, f32[48,128]{1,0:T(8,128)S(1)}, f32[4,48,128]{2,1,0:T(8,128)S(1)}, f32[4,48,128]{2,1,0:T(8,128)S(1)}, ...), condition=%wide.region_61.62_spmd, body=%wide.region_60.61_spmd.sunk | while | flops 884739 | bytes 737377 | solution.py:50
  259.9 5.1 %while.499 = (s32[]{:T(128)}, f32[48,128]{1,0:T(8,128)S(1)}, f32[4,48,128]{2,1,0:T(8,128)S(1)}, f32[4,48,128]{2,1,0:T(8,128)S(1)}, bf16[4,48,48,128]{3,2,1,0:T(8,128)(2,1)}, /*index=5*/s32[]{:T(128)}, s32[]{:T(128)}) while((s32[]{:T(128)}, f32[48,128]{1,0:T(8,128)S(1)}, f32[4,48,128]{2,1,0:T(8,128)S(1)}, f32[4,48,128]{2,1,0:T(8,128)S(1)}, ...), condition=%wide.region_63.64_spmd, body=%wide.region_62.63_spmd.sunk | while | flops 884739 | bytes 737377 | solution.py:50
  270.1 5.1 %while.500 = (s32[]{:T(128)}, f32[48,128]{1,0:T(8,128)S(1)}, f32[4,48,128]{2,1,0:T(8,128)S(1)}, f32[4,48,128]{2,1,0:T(8,128)S(1)}, bf16[4,48,48,128]{3,2,1,0:T(8,128)(2,1)}, /*index=5*/s32[]{:T(128)}, s32[]{:T(128)}) while((s32[]{:T(128)}, f32[48,128]{1,0:T(8,128)S(1)}, f32[4,48,128]{2,1,0:T(8,128)S(1)}, f32[4,48,128]{2,1,0:T(8,128)S(1)}, ...), condition=%wide.region_65.66_spmd, body=%wide.region_64.65_spmd.sunk | while | flops 884739 | bytes 737377 | solution.py:50
  280.4 5.1 %while.501 = (s32[]{:T(128)}, f32[48,128]{1,0:T(8,128)S(1)}, f32[4,48,128]{2,1,0:T(8,128)S(1)}, f32[4,48,128]{2,1,0:T(8,128)S(1)}, bf16[4,48,48,128]{3,2,1,0:T(8,128)(2,1)}, /*index=5*/s32[]{:T(128)}, s32[]{:T(128)}) while((s32[]{:T(128)}, f32[48,128]{1,0:T(8,128)S(1)}, f32[4,48,128]{2,1,0:T(8,128)S(1)}, f32[4,48,128]{2,1,0:T(8,128)S(1)}, ...), condition=%wide.region_67.68_spmd, body=%wide.region_66.67_spmd.sunk | while | flops 884739 | bytes 737377 | solution.py:50
  (476 shorter events, 268.0 us)
Async XLA Ops:
  1.1 6.2 %collective-permute-start.1 = (f32[4,48,2]{2,1,0:T(8,128)S(1)}, f32[4,48,2]{2,1,0:T(8,128)S(1)}, u32[]{:S(2)}, u32[]{:S(2)}) collective-permute-start(f32[4,48,2]{2,1,0:T(8,128)S(1)} %get-tuple-element.2703), channel_id=1, source_target_pairs={{8,0},{16,8},{24,16},{9,1},{17,9},{25,17},{10,2},{18,10},{26,18},{... | collective-permute-start | bytes 4616 | tf_op jit(solution)/shard_map/ppermute | solution.py:22
  4.1 6.3 %collective-permute-start = (f32[4,48,2]{2,1,0:T(8,128)S(1)}, f32[4,48,2]{2,1,0:T(8,128)S(1)}, u32[]{:S(2)}, u32[]{:S(2)}) collective-permute-start(f32[4,48,2]{2,1,0:T(8,128)S(1)} %get-tuple-element.2704), channel_id=1, source_target_pairs={{0,8},{8,16},{16,24},{1,9},{9,17},{17,25},{2,10},{10,18},{18,26},{... | collective-permute-start | bytes 4616 | tf_op jit(solution)/shard_map/ppermute | solution.py:20
  24.7 6.1 %collective-permute-start.2 = (f32[48,128]{1,0:T(8,128)S(1)}, f32[48,128]{1,0:T(8,128)S(1)}, u32[]{:S(2)}, u32[]{:S(2)}) collective-permute-start(f32[48,128]{1,0:T(8,128)S(1)} %slice_bitcast_fusion.27), channel_id=1, source_target_pairs={{0,1},{1,2},{2,3},{3,4},{4,5},{5,6},{6,7},{8,9},{9,10},{10,11},{11... | collective-permute-start | bytes 73736 | tf_op jit(solution)/shard_map/ppermute | solution.py:32
  31.7 5.2 %collective-permute-start.3 = (f32[48,128]{1,0:T(8,128)S(1)}, f32[48,128]{1,0:T(8,128)S(1)}, u32[]{:S(2)}, u32[]{:S(2)}) collective-permute-start(f32[48,128]{1,0:T(8,128)S(1)} %slice_bitcast_fusion.26), channel_id=1, source_target_pairs={{0,1},{1,2},{2,3},{3,4},{4,5},{5,6},{6,7},{8,9},{9,10},{10,11},{11... | collective-permute-start | bytes 73736 | tf_op jit(solution)/shard_map/ppermute | solution.py:32
  37.7 5.2 %collective-permute-start.4 = (f32[48,128]{1,0:T(8,128)S(1)}, f32[48,128]{1,0:T(8,128)S(1)}, u32[]{:S(2)}, u32[]{:S(2)}) collective-permute-start(f32[48,128]{1,0:T(8,128)S(1)} %slice_bitcast_fusion.25), channel_id=1, source_target_pairs={{0,1},{1,2},{2,3},{3,4},{4,5},{5,6},{6,7},{8,9},{9,10},{10,11},{11... | collective-permute-start | bytes 73736 | tf_op jit(solution)/shard_map/ppermute | solution.py:32
  43.7 5.2 %collective-permute-start.5 = (f32[48,128]{1,0:T(8,128)S(1)}, f32[48,128]{1,0:T(8,128)S(1)}, u32[]{:S(2)}, u32[]{:S(2)}) collective-permute-start(f32[48,128]{1,0:T(8,128)S(1)} %slice_bitcast_fusion.24), channel_id=1, source_target_pairs={{0,1},{1,2},{2,3},{3,4},{4,5},{5,6},{6,7},{8,9},{9,10},{10,11},{11... | collective-permute-start | bytes 73736 | tf_op jit(solution)/shard_map/ppermute | solution.py:32
  49.7 5.2 %collective-permute-start.6 = (f32[48,128]{1,0:T(8,128)S(1)}, f32[48,128]{1,0:T(8,128)S(1)}, u32[]{:S(2)}, u32[]{:S(2)}) collective-permute-start(f32[48,128]{1,0:T(8,128)S(1)} %slice_bitcast_fusion.23), channel_id=1, source_target_pairs={{0,1},{1,2},{2,3},{3,4},{4,5},{5,6},{6,7},{8,9},{9,10},{10,11},{11... | collective-permute-start | bytes 73736 | tf_op jit(solution)/shard_map/ppermute | solution.py:32
  55.7 5.2 %collective-permute-start.7 = (f32[48,128]{1,0:T(8,128)S(1)}, f32[48,128]{1,0:T(8,128)S(1)}, u32[]{:S(2)}, u32[]{:S(2)}) collective-permute-start(f32[48,128]{1,0:T(8,128)S(1)} %slice_bitcast_fusion.22), channel_id=1, source_target_pairs={{0,1},{1,2},{2,3},{3,4},{4,5},{5,6},{6,7},{8,9},{9,10},{10,11},{11... | collective-permute-start | bytes 73736 | tf_op jit(solution)/shard_map/ppermute | solution.py:32
  61.7 5.2 %collective-permute-start.8 = (f32[48,128]{1,0:T(8,128)S(1)}, f32[48,128]{1,0:T(8,128)S(1)}, u32[]{:S(2)}, u32[]{:S(2)}) collective-permute-start(f32[48,128]{1,0:T(8,128)S(1)} %slice_bitcast_fusion.21), channel_id=1, source_target_pairs={{0,1},{1,2},{2,3},{3,4},{4,5},{5,6},{6,7},{8,9},{9,10},{10,11},{11... | collective-permute-start | bytes 73736 | tf_op jit(solution)/shard_map/ppermute | solution.py:32
  72.9 5.7 %collective-permute-start.9 = (f32[48,128]{1,0:T(8,128)S(1)}, f32[48,128]{1,0:T(8,128)S(1)}, u32[]{:S(2)}, u32[]{:S(2)}) collective-permute-start(f32[48,128]{1,0:T(8,128)S(1)} %slice_bitcast_fusion.20), channel_id=1, source_target_pairs={{1,0},{2,1},{3,2},{4,3},{5,4},{6,5},{7,6},{9,8},{10,9},{11,10},{12... | collective-permute-start | bytes 73736 | tf_op jit(solution)/shard_map/ppermute | solution.py:32
  94.0 5.1 %collective-permute-start.11 = (f32[48,128]{1,0:T(8,128)S(1)}, f32[48,128]{1,0:T(8,128)S(1)}, u32[]{:S(2)}, u32[]{:S(2)}) collective-permute-start(f32[48,128]{1,0:T(8,128)S(1)} %slice_bitcast_fusion.18), channel_id=1, source_target_pairs={{1,0},{2,1},{3,2},{4,3},{5,4},{6,5},{7,6},{9,8},{10,9},{11,10},{12... | collective-permute-start | bytes 73736 | tf_op jit(solution)/shard_map/ppermute | solution.py:32
  104.2 5.1 %collective-permute-start.12 = (f32[48,128]{1,0:T(8,128)S(1)}, f32[48,128]{1,0:T(8,128)S(1)}, u32[]{:S(2)}, u32[]{:S(2)}) collective-permute-start(f32[48,128]{1,0:T(8,128)S(1)} %slice_bitcast_fusion.17), channel_id=1, source_target_pairs={{1,0},{2,1},{3,2},{4,3},{5,4},{6,5},{7,6},{9,8},{10,9},{11,10},{12... | collective-permute-start | bytes 73736 | tf_op jit(solution)/shard_map/ppermute | solution.py:32
  114.5 5.1 %collective-permute-start.13 = (f32[48,128]{1,0:T(8,128)S(1)}, f32[48,128]{1,0:T(8,128)S(1)}, u32[]{:S(2)}, u32[]{:S(2)}) collective-permute-start(f32[48,128]{1,0:T(8,128)S(1)} %slice_bitcast_fusion.16), channel_id=1, source_target_pairs={{1,0},{2,1},{3,2},{4,3},{5,4},{6,5},{7,6},{9,8},{10,9},{11,10},{12... | collective-permute-start | bytes 73736 | tf_op jit(solution)/shard_map/ppermute | solution.py:32
  145.4 5.4 %collective-permute-start.17 = (f32[4,48,2]{2,1,0:T(8,128)S(1)}, f32[4,48,2]{2,1,0:T(8,128)S(1)}, u32[]{:S(2)}, u32[]{:S(2)}) collective-permute-start(f32[4,48,2]{2,1,0:T(8,128)S(1)} %get-tuple-element.2701), channel_id=1, source_target_pairs={{8,0},{16,8},{24,16},{9,1},{17,9},{25,17},{10,2},{18,10},{26,18},{... | collective-permute-start | bytes 4616 | tf_op jit(solution)/shard_map/ppermute | solution.py:22
  147.3 6.3 %collective-permute-start.16 = (f32[4,48,2]{2,1,0:T(8,128)S(1)}, f32[4,48,2]{2,1,0:T(8,128)S(1)}, u32[]{:S(2)}, u32[]{:S(2)}) collective-permute-start(f32[4,48,2]{2,1,0:T(8,128)S(1)} %get-tuple-element.2702), channel_id=1, source_target_pairs={{0,8},{8,16},{16,24},{1,9},{9,17},{17,25},{2,10},{10,18},{18,26},{... | collective-permute-start | bytes 4616 | tf_op jit(solution)/shard_map/ppermute | solution.py:20
  171.9 5.2 %collective-permute-start.19 = (f32[48,128]{1,0:T(8,128)S(1)}, f32[48,128]{1,0:T(8,128)S(1)}, u32[]{:S(2)}, u32[]{:S(2)}) collective-permute-start(f32[48,128]{1,0:T(8,128)S(1)} %slice_bitcast_fusion.12), channel_id=1, source_target_pairs={{0,1},{1,2},{2,3},{3,4},{4,5},{5,6},{6,7},{8,9},{9,10},{10,11},{11... | collective-permute-start | bytes 73736 | tf_op jit(solution)/shard_map/ppermute | solution.py:32
  177.9 5.2 %collective-permute-start.20 = (f32[48,128]{1,0:T(8,128)S(1)}, f32[48,128]{1,0:T(8,128)S(1)}, u32[]{:S(2)}, u32[]{:S(2)}) collective-permute-start(f32[48,128]{1,0:T(8,128)S(1)} %slice_bitcast_fusion.11), channel_id=1, source_target_pairs={{0,1},{1,2},{2,3},{3,4},{4,5},{5,6},{6,7},{8,9},{9,10},{10,11},{11... | collective-permute-start | bytes 73736 | tf_op jit(solution)/shard_map/ppermute | solution.py:32
  183.9 5.2 %collective-permute-start.21 = (f32[48,128]{1,0:T(8,128)S(1)}, f32[48,128]{1,0:T(8,128)S(1)}, u32[]{:S(2)}, u32[]{:S(2)}) collective-permute-start(f32[48,128]{1,0:T(8,128)S(1)} %slice_bitcast_fusion.10), channel_id=1, source_target_pairs={{0,1},{1,2},{2,3},{3,4},{4,5},{5,6},{6,7},{8,9},{9,10},{10,11},{11... | collective-permute-start | bytes 73736 | tf_op jit(solution)/shard_map/ppermute | solution.py:32
  189.9 5.2 %collective-permute-start.22 = (f32[48,128]{1,0:T(8,128)S(1)}, f32[48,128]{1,0:T(8,128)S(1)}, u32[]{:S(2)}, u32[]{:S(2)}) collective-permute-start(f32[48,128]{1,0:T(8,128)S(1)} %slice_bitcast_fusion.9), channel_id=1, source_target_pairs={{0,1},{1,2},{2,3},{3,4},{4,5},{5,6},{6,7},{8,9},{9,10},{10,11},{11... | collective-permute-start | bytes 73736 | tf_op jit(solution)/shard_map/ppermute | solution.py:32
  195.9 5.2 %collective-permute-start.23 = (f32[48,128]{1,0:T(8,128)S(1)}, f32[48,128]{1,0:T(8,128)S(1)}, u32[]{:S(2)}, u32[]{:S(2)}) collective-permute-start(f32[48,128]{1,0:T(8,128)S(1)} %slice_bitcast_fusion.8), channel_id=1, source_target_pairs={{0,1},{1,2},{2,3},{3,4},{4,5},{5,6},{6,7},{8,9},{9,10},{10,11},{11... | collective-permute-start | bytes 73736 | tf_op jit(solution)/shard_map/ppermute | solution.py:32
  201.9 5.2 %collective-permute-start.24 = (f32[48,128]{1,0:T(8,128)S(1)}, f32[48,128]{1,0:T(8,128)S(1)}, u32[]{:S(2)}, u32[]{:S(2)}) collective-permute-start(f32[48,128]{1,0:T(8,128)S(1)} %slice_bitcast_fusion.7), channel_id=1, source_target_pairs={{0,1},{1,2},{2,3},{3,4},{4,5},{5,6},{6,7},{8,9},{9,10},{10,11},{11... | collective-permute-start | bytes 73736 | tf_op jit(solution)/shard_map/ppermute | solution.py:32
  213.1 5.7 %collective-permute-start.25 = (f32[48,128]{1,0:T(8,128)S(1)}, f32[48,128]{1,0:T(8,128)S(1)}, u32[]{:S(2)}, u32[]{:S(2)}) collective-permute-start(f32[48,128]{1,0:T(8,128)S(1)} %slice_bitcast_fusion.6), channel_id=1, source_target_pairs={{1,0},{2,1},{3,2},{4,3},{5,4},{6,5},{7,6},{9,8},{10,9},{11,10},{12... | collective-permute-start | bytes 73736 | tf_op jit(solution)/shard_map/ppermute | solution.py:32
  223.9 5.1 %collective-permute-start.26 = (f32[48,128]{1,0:T(8,128)S(1)}, f32[48,128]{1,0:T(8,128)S(1)}, u32[]{:S(2)}, u32[]{:S(2)}) collective-permute-start(f32[48,128]{1,0:T(8,128)S(1)} %slice_bitcast_fusion.5), channel_id=1, source_target_pairs={{1,0},{2,1},{3,2},{4,3},{5,4},{6,5},{7,6},{9,8},{10,9},{11,10},{12... | collective-permute-start | bytes 73736 | tf_op jit(solution)/shard_map/ppermute | solution.py:32
  244.4 5.1 %collective-permute-start.28 = (f32[48,128]{1,0:T(8,128)S(1)}, f32[48,128]{1,0:T(8,128)S(1)}, u32[]{:S(2)}, u32[]{:S(2)}) collective-permute-start(f32[48,128]{1,0:T(8,128)S(1)} %slice_bitcast_fusion.3), channel_id=1, source_target_pairs={{1,0},{2,1},{3,2},{4,3},{5,4},{6,5},{7,6},{9,8},{10,9},{11,10},{12... | collective-permute-start | bytes 73736 | tf_op jit(solution)/shard_map/ppermute | solution.py:32
  (12 other events, 81.4 us)
where the time goes:
time: 291 us; the launch traced here: 286 us
  other arithmetic  116 us (40%)
  starting transfers between devices  96.9 us (33%)
  waiting for transfers between devices  65.1 us (22%)
  loops' own time  3.93 us (1%)
  local copies, waits for them, and re-layouts  3.31 us (1%)
    dot_general x144, other arithmetic, matvec(): jnp.einsum('abs,bs->as', block.astype(jnp.float32), vector, precision=HIGH)  112 us
    ppermute x28, starting transfers between devices, passed_along(): return lax.ppermute(value, axis, pairs)  86.3 us
    ppermute x28, waiting for transfers between devices, passed_along(): return lax.ppermute(value, axis, pairs)  59.1 us
    ppermute x2, waiting for transfers between devices, with_halo(): lax.ppermute(tail, axis, [(i, (i + 1) % count) for i in range(ends)])  5.94 us
  transfers between devices with their start and end apart: 32, of which 30 were waited for; matrix products, arithmetic and copies ran while one was open for 0% of the time, Pallas kernels for 0%

commit v1 on v0

v1 whole, which is shorter than its diff:
```python
import functools

import jax
import jax.numpy as jnp
from jax import lax
from jax.experimental import pallas as pl
from jax.experimental.pallas import tpu as pltpu
from jax.sharding import PartitionSpec as P

SWEEPS = 2
ROWS = 8
EDGE = 2
F32 = jnp.float32


def row_sums(regs):
    row = lax.broadcasted_iota(jnp.int32, regs[0].shape, 0)
    for half in (4, 2, 1):
        low = (row % (2 * half)) < half
        merged = []
        for i in range(half):
            a, b = regs[i], regs[i + half]
            keep = jnp.where(low, a, b)
            move = jnp.where(low, b, a)
            if half == 4:
                moved = pltpu.roll(move, half, 0)
            else:
                moved = jnp.where(
                    low, pltpu.roll(move, ROWS - half, 0), pltpu.roll(move, half, 0)
                )
            merged.append(keep + moved)
        regs = merged
    return regs[0]


def matvec(block_ref, cell, vector):
    equations = vector.shape[0]
    out = []
    for group in range(equations // ROWS):
        regs = []
        for a in range(ROWS):
            product = block_ref[cell, group * ROWS + a].astype(F32) * vector
            parts = [product[i : i + ROWS] for i in range(0, equations, ROWS)]
            while len(parts) > 1:
                parts = [
                    parts[i] + parts[i + 1] if i + 1 < len(parts) else parts[i]
                    for i in range(0, len(parts), 2)
                ]
            regs.append(parts[0])
        out.append(row_sums(regs))
    return jnp.concatenate(out, axis=0)


def pack_edges(cell):
    equations, width = cell.shape
    lane = lax.broadcasted_iota(jnp.int32, (ROWS, width), 1)
    packed = jnp.zeros((ROWS, width), F32)
    for g in range(equations // ROWS):
        moved = pltpu.roll(cell[g * ROWS : (g + 1) * ROWS], EDGE + 2 * EDGE * g, 1)
        packed = jnp.where(lane // (2 * EDGE) == g, moved, packed)
    return packed


def unpack_edges(packed, equations):
    width = packed.shape[1]
    return jnp.concatenate(
        [
            pltpu.roll(packed, width - EDGE - 2 * EDGE * g, 1)
            for g in range(equations // ROWS)
        ],
        axis=0,
    )


def kernel(
    rhs_h, prev_h, minus_h, plus_h, diss_h, inv_h, low_h, up_h, out_h,
    rhs, delta, minus, plus, diss, inv, low, up, source, line,
    edge_out, edge_in, carry_out, carry_in,
    load_sem, block_sem, store_sem, edge_send, edge_recv, carry_send, carry_recv,
):
    cells, equations, width = rhs.shape
    norm, surf = lax.axis_index("norm"), lax.axis_index("surf")
    norms, surfs = lax.axis_size("norm"), lax.axis_size("surf")
    has_below, has_above = norm > 0, norm < norms - 1
    has_left, has_right = surf > 0, surf < surfs - 1

    small = [
        pltpu.make_async_copy(src, dst, load_sem.at[i])
        for i, (src, dst) in enumerate(((prev_h, delta), (rhs_h, rhs), (diss_h, diss)))
    ]
    pairs = ((minus_h, minus), (plus_h, plus), (inv_h, inv), (low_h, low), (up_h, up))

    def block_copy(kind, cell):
        src, dst = pairs[kind]
        return pltpu.make_async_copy(src.at[cell], dst.at[cell], block_sem.at[kind, cell])

    for copy in small:
        copy.start()
    for cell in range(cells):
        for kind in range(3):
            block_copy(kind, cell).start()
    for cell in range(cells):
        block_copy(3, cell).start()
    for cell in reversed(range(cells)):
        block_copy(4, cell).start()

    neighbours = (
        (has_below, {"norm": norm - 1}),
        (has_above, {"norm": norm + 1}),
        (has_left, {"surf": surf - 1}),
        (has_right, {"surf": surf + 1}),
    )
    barrier = pltpu.get_barrier_semaphore()
    for present, where in neighbours:
        @pl.when(present)
        def _():
            pl.semaphore_signal(
                barrier, inc=1, device_id=where, device_id_type=pl.DeviceIdType.MESH
            )

    @pl.when(jnp.logical_not(has_left))
    def _():
        edge_in[:, 0] = jnp.zeros_like(edge_in[:, 0])

    @pl.when(jnp.logical_not(has_right))
    def _():
        edge_in[:, 1] = jnp.zeros_like(edge_in[:, 1])

    @pl.when(jnp.logical_not(has_below))
    def _():
        for sweep in range(SWEEPS):
            carry_in[2 * sweep] = jnp.zeros((equations, width), F32)

    @pl.when(jnp.logical_not(has_above))
    def _():
        for sweep in range(SWEEPS):
            carry_in[2 * sweep + 1] = jnp.zeros((equations, width), F32)

    pl.semaphore_wait(barrier, sum(present.astype(jnp.int32) for present, _ in neighbours))

    def edge_copy(sweep, side, cell):
        return pltpu.make_async_remote_copy(
            src_ref=edge_out.at[sweep, cell],
            dst_ref=edge_in.at[sweep, side, cell],
            send_sem=edge_send.at[sweep, side, cell],
            recv_sem=edge_recv.at[sweep, side, cell],
            device_id={"surf": surf + 1 - 2 * side},
            device_id_type=pl.DeviceIdType.MESH,
        )

    def carry_copy(index):
        return pltpu.make_async_remote_copy(
            src_ref=carry_out.at[index],
            dst_ref=carry_in.at[index],
            send_sem=carry_send.at[index],
            recv_sem=carry_recv.at[index],
            device_id={"norm": norm + 1 - 2 * (index % 2)},
            device_id_type=pl.DeviceIdType.MESH,
        )

    def send_edges(sweep, cell, value):
        edge_out[sweep, cell] = pack_edges(value)

        @pl.when(has_right)
        def _():
            edge_copy(sweep, 0, cell).start()

        @pl.when(has_left)
        def _():
            edge_copy(sweep, 1, cell).start()

    lane = lax.broadcasted_iota(jnp.int32, (equations, width), 1)

    def source_cell(sweep, cell):
        @pl.when(has_left)
        def _():
            edge_copy(sweep, 0, cell).wait_recv()

        @pl.when(has_right)
        def _():
            edge_copy(sweep, 1, cell).wait_recv()

        if sweep == 0:
            for kind in range(3):
                block_copy(kind, cell).wait()
        centre = delta[cell]
        left = unpack_edges(edge_in[sweep, 0, cell], equations)
        right = unpack_edges(edge_in[sweep, 1, cell], equations)
        left_one = pltpu.roll(jnp.where(lane == width - 1, left, centre), 1, 1)
        left_two = pltpu.roll(jnp.where(lane >= width - 2, left, centre), 2, 1)
        right_one = pltpu.roll(jnp.where(lane == 0, right, centre), width - 1, 1)
        right_two = pltpu.roll(jnp.where(lane <= 1, right, centre), width - 2, 1)
        fourth = left_two - 4.0 * left_one + 6.0 * centre - 4.0 * right_one + right_two
        residual = rhs[cell] - diss[cell] * fourth
        residual = residual - matvec(minus, cell, left_one)
        residual = residual - matvec(plus, cell, right_one)
        source[cell] = matvec(inv, cell, residual)

    small[0].wait()

    def first_edges(cell, _):
        send_edges(0, cell, delta[cell])
        return 0

    lax.fori_loop(0, cells, first_edges, 0)
    small[1].wait()
    small[2].wait()

    for sweep in range(SWEEPS):
        last_sweep = sweep == SWEEPS - 1

        def source_step(step, _):
            source_cell(sweep, step if sweep == 0 else cells - 1 - step)
            return 0

        lax.fori_loop(0, cells, source_step, 0)

        def forward_step(cell, carry):
            value = source[cell] + matvec(low, cell, carry)
            line[cell] = value
            return value

        def backward_step(step, carry):
            cell = cells - 1 - step
            value = line[cell] + matvec(up, cell, carry)
            delta[cell] = value
            if last_sweep:
                pltpu.make_async_copy(delta.at[cell], out_h.at[cell], store_sem.at[cell]).start()
            else:
                send_edges(sweep + 1, cell, value)
            return value

        for index, step, arrives, leaves, kind in (
            (2 * sweep, forward_step, has_below, has_above, 3),
            (2 * sweep + 1, backward_step, has_above, has_below, 4),
        ):
            if sweep == 0:
                for cell in range(cells):
                    block_copy(kind, cell).wait()

            @pl.when(arrives)
            def _():
                carry_copy(index).wait_recv()

            carry = lax.fori_loop(0, cells, step, carry_in[index])

            @pl.when(leaves)
            def _():
                carry_out[index] = carry
                carry_copy(index).start()

    for cell in range(cells):
        pltpu.make_async_copy(delta.at[cell], out_h.at[cell], store_sem.at[cell]).wait()
    for sweep in range(SWEEPS):
        for cell in range(cells):
            for side, present in ((0, has_right), (1, has_left)):
                @pl.when(present)
                def _():
                    edge_copy(sweep, side, cell).wait_send()

        for index, leaves in ((2 * sweep, has_above), (2 * sweep + 1, has_below)):
            @pl.when(leaves)
            def _():
                carry_copy(index).wait_send()


def shards(*arrays):
    cells, equations, width = arrays[0].shape
    vector = pltpu.VMEM((cells, equations, width), F32)
    matrix = pltpu.VMEM((cells, equations, equations, width), jnp.bfloat16)
    dma = pltpu.SemaphoreType.DMA
    return pl.pallas_call(
        kernel,
        out_shape=jax.ShapeDtypeStruct((cells, equations, width), F32),
        in_specs=[pl.BlockSpec(memory_space=pl.ANY)] * len(arrays),
        out_specs=pl.BlockSpec(memory_space=pl.ANY),
        scratch_shapes=[
            vector, vector, matrix, matrix, vector, matrix, matrix, matrix, vector, vector,
            pltpu.VMEM((SWEEPS, cells, ROWS, width), F32),
            pltpu.VMEM((SWEEPS, 2, cells, ROWS, width), F32),
            pltpu.VMEM((2 * SWEEPS, equations, width), F32),
            pltpu.VMEM((2 * SWEEPS, equations, width), F32),
            dma((3,)), dma((5, cells)), dma((cells,)),
            dma((SWEEPS, 2, cells)), dma((SWEEPS, 2, cells)),
            dma((2 * SWEEPS,)), dma((2 * SWEEPS,)),
        ],
        compiler_params=pltpu.CompilerParams(
            collective_id=0, has_side_effects=True, vmem_limit_bytes=56 * 1024 * 1024
        ),
        name="line_relaxation",
    )(*arrays)


def solution(mesh):
    vectors = P("norm", None, "surf")
    blocks = P("norm", None, None, "surf")
    return jax.shard_map(
        shards,
        mesh=mesh,
        in_specs=(vectors, vectors, blocks, blocks, vectors, blocks, blocks, blocks),
        out_specs=vectors,
        check_vma=False,
    )
```

time: 291 us -> 82.8 us (0.28)
  the two profiles are of different devices: /device:TPU:5 before, /device:TPU:0 now
where the time goes in v1:
time: 82.8 us; the launch traced here: 82.7 us
  Pallas kernels  81.1 us (98%)
  local copies, waits for them, and re-layouts  1.54 us (2%)
    pallas_call x1, Pallas kernels, shards(): pl.pallas_call(kernel, out_shape=jax.ShapeDtypeStruct((cells, equations,...  81.1 us

profile of v1, /device:TPU:0, one launch (start us, length us, event | category | flops | bytes accessed | tf_op | source)
XLA Modules:
  0.0 82.7 jit_solution(3210141789146068987)
XLA Ops:
  0.0 81.1 %line_relaxation.1 = f32[4,48,128]{2,1,0:T(8,128)} custom-call(f32[4,48,128]{2,1,0:T(8,128)} %rhs_h.1, f32[4,48,128]{2,1,0:T(8,128)} %prev_h.1, bf16[4,48,48,128]{3,2,1,0:T(8,128)(2,1)} %minus_h.1, bf16[4,48,48,128]{3,2,1,0:T(8,128)(2,1)} %plus_h.1, f32[4,48,128]{2,1,0:T(8,128)} %diss_h.1, bf16[4,48,48,128]{3,2,1,0:T(8,128)(2,1)} %inv_h.1, ...), custom_call_target="tpu_custom_call" | custom-call | tf_op jit(solution)/shard_map/line_relaxation/pallas_call | solution.py:272
  81.1 1.5 %copy.10 = f32[4,48,128]{2,1,0:T(8,128)} copy(f32[4,48,128]{2,1,0:T(8,128)} %line_relaxation.1) | data formatting | bytes 196608

commit v2 on v1

--- a/solution.py
+++ b/solution.py
@@ -10,6 +10,7 @@
 SWEEPS = 2
 ROWS = 8
 EDGE = 2
+CHUNK = 16
 F32 = jnp.float32
 
 
@@ -33,7 +34,7 @@
     return regs[0]
 
 
-def matvec(block_ref, cell, vector):
+def matvec(block_ref, cell, vector, each_group=None):
     equations = vector.shape[0]
     out = []
     for group in range(equations // ROWS):
@@ -48,6 +49,8 @@
                 ]
             regs.append(parts[0])
         out.append(row_sums(regs))
+        if each_group is not None:
+            each_group(group, out[-1])
     return jnp.concatenate(out, axis=0)
 
 
@@ -75,7 +78,7 @@
 def kernel(
     rhs_h, prev_h, minus_h, plus_h, diss_h, inv_h, low_h, up_h, out_h,
     rhs, delta, minus, plus, diss, inv, low, up, source, line,
-    edge_out, edge_in, carry_out, carry_in,
+    edge_out, edge_in, carry_out, carry_in, low_wide, up_wide,
     load_sem, block_sem, store_sem, edge_send, edge_recv, carry_send, carry_recv,
 ):
     cells, equations, width = rhs.shape
@@ -126,16 +129,6 @@
     def _():
         edge_in[:, 1] = jnp.zeros_like(edge_in[:, 1])
 
-    @pl.when(jnp.logical_not(has_below))
-    def _():
-        for sweep in range(SWEEPS):
-            carry_in[2 * sweep] = jnp.zeros((equations, width), F32)
-
-    @pl.when(jnp.logical_not(has_above))
-    def _():
-        for sweep in range(SWEEPS):
-            carry_in[2 * sweep + 1] = jnp.zeros((equations, width), F32)
-
     pl.semaphore_wait(barrier, sum(present.astype(jnp.int32) for present, _ in neighbours))
 
     def edge_copy(sweep, side, cell):
@@ -148,15 +141,28 @@
             device_id_type=pl.DeviceIdType.MESH,
         )
 
-    def carry_copy(index):
+    def carry_copy(index, chunk):
+        rows = pl.ds(chunk * CHUNK, CHUNK)
         return pltpu.make_async_remote_copy(
-            src_ref=carry_out.at[index],
-            dst_ref=carry_in.at[index],
-            send_sem=carry_send.at[index],
-            recv_sem=carry_recv.at[index],
+            src_ref=carry_out.at[index, rows],
+            dst_ref=carry_in.at[index, rows],
+            send_sem=carry_send.at[index, chunk],
+            recv_sem=carry_recv.at[index, chunk],
             device_id={"norm": norm + 1 - 2 * (index % 2)},
             device_id_type=pl.DeviceIdType.MESH,
         )
+
+    def widen(kind, wide):
+        def rows(step, _):
+            cell, group = step // (equations // ROWS), step % (equations // ROWS)
+            for a in range(ROWS):
+                row = group * ROWS + a
+                wide[cell, row] = pairs[kind][1][cell, row].astype(F32)
+            return 0
+
+        for cell in range(cells):
+            block_copy(kind, cell).wait()
+        lax.fori_loop(0, cells * (equations // ROWS), rows, 0)
 
     def send_edges(sweep, cell, value):
         edge_out[sweep, cell] = pack_edges(value)
@@ -215,39 +221,75 @@
 
         lax.fori_loop(0, cells, source_step, 0)
 
-        def forward_step(cell, carry):
-            value = source[cell] + matvec(low, cell, carry)
-            line[cell] = value
-            return value
-
-        def backward_step(step, carry):
-            cell = cells - 1 - step
-            value = line[cell] + matvec(up, cell, carry)
-            delta[cell] = value
+        def run_pass(index, arrives, leaves, blocks, given, result, finish):
+            backward = index % 2
+            place = lambda step: cells - 1 - step if backward else step
+
+            @pl.when(arrives)
+            def _():
+                for chunk in range(equations // CHUNK):
+                    carry_copy(index, chunk).wait_recv()
+
+            @pl.when(jnp.logical_not(arrives))
+            def _():
+                first = given[place(0)]
+                carry_in[index] = first
+                result[place(0)] = first
+                finish(place(0), first)
+
+            def step_cell(step, carry):
+                cell = place(step)
+                value = given[cell] + matvec(blocks, cell, carry)
+                result[cell] = value
+                finish(cell, value)
+                return value
+
+            begin = 1 - arrives.astype(jnp.int32)
+            carry = lax.fori_loop(begin, cells - 1, step_cell, carry_in[index])
+            last = place(cells - 1)
+
+            @pl.when(leaves)
+            def _():
+                def send_group(group, sums):
+                    rows = slice(group * ROWS, (group + 1) * ROWS)
+                    carry_out[index, rows] = given[last, rows] + sums
+                    if (group + 1) * ROWS % CHUNK == 0:
+                        carry_copy(index, group * ROWS // CHUNK).start()
+
+                matvec(blocks, last, carry, send_group)
+                value = carry_out[index]
+                result[last] = value
+                finish(last, value)
+
+            @pl.when(jnp.logical_not(leaves))
+            def _():
+                value = given[last] + matvec(blocks, last, carry)
+                result[last] = value
+                finish(last, value)
+
+        def keep(cell, value):
+            pass
+
+        def pass_on(cell, value):
             if last_sweep:
                 pltpu.make_async_copy(delta.at[cell], out_h.at[cell], store_sem.at[cell]).start()
             else:
                 send_edges(sweep + 1, cell, value)
-            return value
-
-        for index, step, arrives, leaves, kind in (
-            (2 * sweep, forward_step, has_below, has_above, 3),
-            (2 * sweep + 1, backward_step, has_above, has_below, 4),
-        ):
-            if sweep == 0:
-                for cell in range(cells):
-                    block_copy(kind, cell).wait()
-
-            @pl.when(arrives)
-            def _():
-                carry_copy(index).wait_recv()
-
-            carry = lax.fori_loop(0, cells, step, carry_in[index])
-
-            @pl.when(leaves)
-            def _():
-                carry_out[index] = carry
-                carry_copy(index).start()
+
+        if sweep == 0:
+            widen(3, low_wide)
+
+            @pl.when(has_below)
+            def _():
+                widen(4, up_wide)
+
+        run_pass(2 * sweep, has_below, has_above, low_wide, source, line, keep)
+        if sweep == 0:
+            @pl.when(jnp.logical_not(has_below))
+            def _():
+                widen(4, up_wide)
+
+        run_pass(2 * sweep + 1, has_above, has_below, up_wide, line, delta, pass_on)
 
     for cell in range(cells):
         pltpu.make_async_copy(delta.at[cell], out_h.at[cell], store_sem.at[cell]).wait()
@@ -261,13 +303,15 @@
         for index, leaves in ((2 * sweep, has_above), (2 * sweep + 1, has_below)):
             @pl.when(leaves)
             def _():
-                carry_copy(index).wait_send()
+                for chunk in range(equations // CHUNK):
+                    carry_copy(index, chunk).wait_send()
 
 
 def shards(*arrays):
     cells, equations, width = arrays[0].shape
     vector = pltpu.VMEM((cells, equations, width), F32)
     matrix = pltpu.VMEM((cells, equations, equations, width), jnp.bfloat16)
+    wide = pltpu.VMEM((cells, equations, equations, width), F32)
     dma = pltpu.SemaphoreType.DMA
     return pl.pallas_call(
         kernel,
@@ -280,9 +324,10 @@
             pltpu.VMEM((SWEEPS, 2, cells, ROWS, width), F32),
             pltpu.VMEM((2 * SWEEPS, equations, width), F32),
             pltpu.VMEM((2 * SWEEPS, equations, width), F32),
+            wide, wide,
             dma((3,)), dma((5, cells)), dma((cells,)),
             dma((SWEEPS, 2, cells)), dma((SWEEPS, 2, cells)),
-            dma((2 * SWEEPS,)), dma((2 * SWEEPS,)),
+            dma((2 * SWEEPS, equations // CHUNK)), dma((2 * SWEEPS, equations // CHUNK)),
         ],
         compiler_params=pltpu.CompilerParams(
             collective_id=0, has_side_effects=True, vmem_limit_bytes=56 * 1024 * 1024

time: 82.8 us -> 77.3 us (0.934)
  Pallas kernels: 81.1 us -> 75.6 us
    pallas_call x1, Pallas kernels: 81.1 us -> 75.6 us  [shards(): pl.pallas_call(kernel, out_shape=jax.ShapeDtypeStruct((cells, equations,...]
where the time goes in v2:
time: 77.3 us; the launch traced here: 77.1 us
  Pallas kernels  75.6 us (98%)
  local copies, waits for them, and re-layouts  1.54 us (2%)
    pallas_call x1, Pallas kernels, shards(): pl.pallas_call(kernel, out_shape=jax.ShapeDtypeStruct((cells, equations,...  75.6 us

profile of v2, /device:TPU:0, one launch (start us, length us, event | category | flops | bytes accessed | tf_op | source)
XLA Modules:
  0.0 77.1 jit_solution(5214316153840697302)
XLA Ops:
  0.0 75.6 %line_relaxation.1 = f32[4,48,128]{2,1,0:T(8,128)} custom-call(f32[4,48,128]{2,1,0:T(8,128)} %rhs_h.1, f32[4,48,128]{2,1,0:T(8,128)} %prev_h.1, bf16[4,48,48,128]{3,2,1,0:T(8,128)(2,1)} %minus_h.1, bf16[4,48,48,128]{3,2,1,0:T(8,128)(2,1)} %plus_h.1, f32[4,48,128]{2,1,0:T(8,128)} %diss_h.1, bf16[4,48,48,128]{3,2,1,0:T(8,128)(2,1)} %inv_h.1, ...), custom_call_target="tpu_custom_call" | custom-call | tf_op jit(solution)/shard_map/line_relaxation/pallas_call | solution.py:316
  75.6 1.5 %copy.10 = f32[4,48,128]{2,1,0:T(8,128)} copy(f32[4,48,128]{2,1,0:T(8,128)} %line_relaxation.1) | data formatting | bytes 196608

commit v3 on v2

--- a/solution.py
+++ b/solution.py
@@ -11,6 +11,7 @@
 ROWS = 8
 EDGE = 2
 CHUNK = 16
+TILE = 4
 F32 = jnp.float32
 
 
@@ -78,7 +79,7 @@
 def kernel(
     rhs_h, prev_h, minus_h, plus_h, diss_h, inv_h, low_h, up_h, out_h,
     rhs, delta, minus, plus, diss, inv, low, up, source, line,
-    edge_out, edge_in, carry_out, carry_in, low_wide, up_wide,
+    edge_out, edge_in, carry_out, carry_in, wide, joined, local_out,
     load_sem, block_sem, store_sem, edge_send, edge_recv, carry_send, carry_recv,
 ):
     cells, equations, width = rhs.shape
@@ -152,17 +153,44 @@
             device_id_type=pl.DeviceIdType.MESH,
         )
 
-    def widen(kind, wide):
+    def widen(kind):
         def rows(step, _):
             cell, group = step // (equations // ROWS), step % (equations // ROWS)
             for a in range(ROWS):
                 row = group * ROWS + a
-                wide[cell, row] = pairs[kind][1][cell, row].astype(F32)
+                wide[kind - 3, cell, row] = pairs[kind][1][cell, row].astype(F32)
             return 0
 
         for cell in range(cells):
             block_copy(kind, cell).wait()
         lax.fori_loop(0, cells * (equations // ROWS), rows, 0)
+
+    def join(unit, _):
+        kind, step = unit // (cells - 1), unit % (cells - 1)
+        cell = (step + 1) * (1 - kind) + (cells - 2 - step) * kind
+        made, used = step % 2, (step + 1) % 2
+
+        @pl.when(step == 0)
+        def _():
+            def copy_row(row, _):
+                joined[kind, 1, row] = wide[kind, (cells - 1) * kind, row]
+                return 0
+
+            lax.fori_loop(0, equations, copy_row, 0)
+
+        def rows(group, _):
+            tile = pl.ds(group * TILE, TILE)
+            total = jnp.zeros((TILE, equations, width), F32)
+            for b in range(equations):
+                total += wide[kind, cell, tile, b : b + 1, :] * joined[kind, used, b][None]
+            joined[kind, made, tile] = total
+            return 0
+
+        lax.fori_loop(0, equations // TILE, rows, 0)
+        return 0
+
+    units = 2 * (cells - 1)
+    early_units = jnp.minimum(units, norms - 1 - norm)
 
     def send_edges(sweep, cell, value):
         edge_out[sweep, cell] = pack_edges(value)
@@ -267,6 +295,46 @@
                 result[last] = value
                 finish(last, value)
 
+        def run_joined(index, arrives, leaves, blocks, given, result, finish):
+            backward = index % 2
+            place = lambda step: cells - 1 - step if backward else step
+            middle = jnp.logical_and(arrives, leaves)
+            last = place(cells - 1)
+
+            @pl.when(middle)
+            def _():
+                def local_step(step, carry):
+                    cell = place(step)
+                    return given[cell] + matvec(blocks, cell, carry)
+
+                local_out[...] = lax.fori_loop(1, cells, local_step, given[place(0)])
+                for chunk in range(equations // CHUNK):
+                    carry_copy(index, chunk).wait_recv()
+
+                def send_group(group, sums):
+                    rows = slice(group * ROWS, (group + 1) * ROWS)
+                    carry_out[index, rows] = local_out[rows] + sums
+                    if (group + 1) * ROWS % CHUNK == 0:
+                        carry_copy(index, group * ROWS // CHUNK).start()
+
+                matvec(joined.at[backward], cells % 2, carry_in[index], send_group)
+
+                def step_cell(step, carry):
+                    cell = place(step)
+                    value = given[cell] + matvec(blocks, cell, carry)
+                    result[cell] = value
+                    finish(cell, value)
+                    return value
+
+                lax.fori_loop(0, cells - 1, step_cell, carry_in[index])
+                value = carry_out[index]
+                result[last] = value
+                finish(last, value)
+
+            @pl.when(jnp.logical_not(middle))
+            def _():
+                run_pass(index, arrives, leaves, blocks, given, result, finish)
+
         def keep(cell, value):
             pass
 
@@ -277,19 +345,24 @@
                 send_edges(sweep + 1, cell, value)
 
         if sweep == 0:
-            widen(3, low_wide)
+            widen(3)
 
             @pl.when(has_below)
             def _():
-                widen(4, up_wide)
-
-        run_pass(2 * sweep, has_below, has_above, low_wide, source, line, keep)
+                widen(4)
+
+        run = run_pass if sweep == 0 else run_joined
+        if sweep == 1:
+            lax.fori_loop(early_units, units, join, 0)
+        run(2 * sweep, has_below, has_above, wide.at[0], source, line, keep)
         if sweep == 0:
             @pl.when(jnp.logical_not(has_below))
             def _():
-                widen(4, up_wide)
-
-        run_pass(2 * sweep + 1, has_above, has_below, up_wide, line, delta, pass_on)
+                widen(4)
+
+            lax.fori_loop(0, early_units, join, 0)
+
+        run(2 * sweep + 1, has_above, has_below, wide.at[1], line, delta, pass_on)
 
     for cell in range(cells):
         pltpu.make_async_copy(delta.at[cell], out_h.at[cell], store_sem.at[cell]).wait()
@@ -311,7 +384,6 @@
     cells, equations, width = arrays[0].shape
     vector = pltpu.VMEM((cells, equations, width), F32)
     matrix = pltpu.VMEM((cells, equations, equations, width), jnp.bfloat16)
-    wide = pltpu.VMEM((cells, equations, equations, width), F32)
     dma = pltpu.SemaphoreType.DMA
     return pl.pallas_call(
         kernel,
@@ -324,7 +396,9 @@
             pltpu.VMEM((SWEEPS, 2, cells, ROWS, width), F32),
             pltpu.VMEM((2 * SWEEPS, equations, width), F32),
             pltpu.VMEM((2 * SWEEPS, equations, width), F32),
-            wide, wide,
+            pltpu.VMEM((2, cells, equations, equations, width), F32),
+            pltpu.VMEM((2, 2, equations, equations, width), F32),
+            pltpu.VMEM((equations, width), F32),
             dma((3,)), dma((5, cells)), dma((cells,)),
             dma((SWEEPS, 2, cells)), dma((SWEEPS, 2, cells)),
             dma((2 * SWEEPS, equations // CHUNK)), dma((2 * SWEEPS, equations // CHUNK)),

time: 77.3 us -> 74.6 us (0.965)
  Pallas kernels: 75.6 us -> 72.9 us
    pallas_call x1, Pallas kernels: 75.6 us -> 72.9 us  [shards(): pl.pallas_call(kernel, out_shape=jax.ShapeDtypeStruct((cells, equations,...]
where the time goes in v3:
time: 74.6 us; the launch traced here: 74.5 us
  Pallas kernels  72.9 us (98%)
  local copies, waits for them, and re-layouts  1.54 us (2%)
    pallas_call x1, Pallas kernels, shards(): pl.pallas_call(kernel, out_shape=jax.ShapeDtypeStruct((cells, equations,...  72.9 us
    unnamed x1, local copies, waits for them, and re-layouts  1.54 us

profile of v3, /device:TPU:0, one launch (start us, length us, event | category | flops | bytes accessed | tf_op | source)
XLA Modules:
  0.0 74.5 jit_solution(10962186076151179274)
XLA Ops:
  0.0 72.9 %line_relaxation.1 = f32[4,48,128]{2,1,0:T(8,128)} custom-call(f32[4,48,128]{2,1,0:T(8,128)} %rhs_h.1, f32[4,48,128]{2,1,0:T(8,128)} %prev_h.1, bf16[4,48,48,128]{3,2,1,0:T(8,128)(2,1)} %minus_h.1, bf16[4,48,48,128]{3,2,1,0:T(8,128)(2,1)} %plus_h.1, f32[4,48,128]{2,1,0:T(8,128)} %diss_h.1, bf16[4,48,48,128]{3,2,1,0:T(8,128)(2,1)} %inv_h.1, ...), custom_call_target="tpu_custom_call" | custom-call | tf_op jit(solution)/shard_map/line_relaxation/pallas_call | solution.py:388
  72.9 1.5 %copy.10 = f32[4,48,128]{2,1,0:T(8,128)} copy(f32[4,48,128]{2,1,0:T(8,128)} %line_relaxation.1) | data formatting | bytes 196608

commit v4 on v3

--- a/solution.py
+++ b/solution.py
@@ -189,8 +189,10 @@
         lax.fori_loop(0, equations // TILE, rows, 0)
         return 0
 
-    units = 2 * (cells - 1)
-    early_units = jnp.minimum(units, norms - 1 - norm)
+    units = 2 * (cells - 1) * jnp.logical_and(has_below, has_above).astype(jnp.int32)
+    done_0 = jnp.minimum(units, jnp.maximum(0, (norm - 2) // 2))
+    done_1 = jnp.minimum(units, done_0 + (norms - 1 - norm) * 7 // 10)
+    done_2 = jnp.minimum(units, jnp.maximum(done_1 + norm * 7 // 10, cells - 1))
 
     def send_edges(sweep, cell, value):
         edge_out[sweep, cell] = pack_edges(value)
@@ -351,16 +353,20 @@
             def _():
                 widen(4)
 
+            lax.fori_loop(0, done_0, join, 0)
+
         run = run_pass if sweep == 0 else run_joined
         if sweep == 1:
-            lax.fori_loop(early_units, units, join, 0)
+            lax.fori_loop(done_1, done_2, join, 0)
         run(2 * sweep, has_below, has_above, wide.at[0], source, line, keep)
         if sweep == 0:
             @pl.when(jnp.logical_not(has_below))
             def _():
                 widen(4)
 
-            lax.fori_loop(0, early_units, join, 0)
+            lax.fori_loop(done_0, done_1, join, 0)
+        else:
+            lax.fori_loop(done_2, units, join, 0)
 
         run(2 * sweep + 1, has_above, has_below, wide.at[1], line, delta, pass_on)
 

time: 74.6 us -> 73.4 us (0.984)
  Pallas kernels: 72.9 us -> 71.7 us
    pallas_call x1, Pallas kernels: 72.9 us -> 71.7 us  [shards(): pl.pallas_call(kernel, out_shape=jax.ShapeDtypeStruct((cells, equations,...]
where the time goes in v4:
time: 73.4 us; the launch traced here: 73.2 us
  Pallas kernels  71.7 us (98%)
  local copies, waits for them, and re-layouts  1.54 us (2%)
    pallas_call x1, Pallas kernels, shards(): pl.pallas_call(kernel, out_shape=jax.ShapeDtypeStruct((cells, equations,...  71.7 us
    unnamed x1, local copies, waits for them, and re-layouts  1.54 us

profile of v4, /device:TPU:0, one launch (start us, length us, event | category | flops | bytes accessed | tf_op | source)
XLA Modules:
  0.0 73.2 jit_solution(14509193306157513924)
XLA Ops:
  0.0 71.7 %line_relaxation.1 = f32[4,48,128]{2,1,0:T(8,128)} custom-call(f32[4,48,128]{2,1,0:T(8,128)} %rhs_h.1, f32[4,48,128]{2,1,0:T(8,128)} %prev_h.1, bf16[4,48,48,128]{3,2,1,0:T(8,128)(2,1)} %minus_h.1, bf16[4,48,48,128]{3,2,1,0:T(8,128)(2,1)} %plus_h.1, f32[4,48,128]{2,1,0:T(8,128)} %diss_h.1, bf16[4,48,48,128]{3,2,1,0:T(8,128)(2,1)} %inv_h.1, ...), custom_call_target="tpu_custom_call" | custom-call | tf_op jit(solution)/shard_map/line_relaxation/pallas_call | solution.py:394
  71.7 1.5 %copy.10 = f32[4,48,128]{2,1,0:T(8,128)} copy(f32[4,48,128]{2,1,0:T(8,128)} %line_relaxation.1) | data formatting | bytes 196608

commit v5 on v4

--- a/solution.py
+++ b/solution.py
@@ -10,7 +10,7 @@
 SWEEPS = 2
 ROWS = 8
 EDGE = 2
-CHUNK = 16
+CHUNK = 24
 TILE = 4
 F32 = jnp.float32
 

time: 73.4 us -> 73.4 us (level)
  no operation moved by 1% of the time
where the time goes in v5:
time: 73.4 us; the launch traced here: 73.3 us
  Pallas kernels  71.7 us (98%)
  local copies, waits for them, and re-layouts  1.54 us (2%)
    pallas_call x1, Pallas kernels, shards(): pl.pallas_call(kernel, out_shape=jax.ShapeDtypeStruct((cells, equations,...  71.7 us
    unnamed x1, local copies, waits for them, and re-layouts  1.54 us

profile of v5, /device:TPU:0, one launch (start us, length us, event | category | flops | bytes accessed | tf_op | source)
XLA Modules:
  0.0 73.3 jit_solution(17019406182425150944)
XLA Ops:
  0.0 71.7 %line_relaxation.1 = f32[4,48,128]{2,1,0:T(8,128)} custom-call(f32[4,48,128]{2,1,0:T(8,128)} %rhs_h.1, f32[4,48,128]{2,1,0:T(8,128)} %prev_h.1, bf16[4,48,48,128]{3,2,1,0:T(8,128)(2,1)} %minus_h.1, bf16[4,48,48,128]{3,2,1,0:T(8,128)(2,1)} %plus_h.1, f32[4,48,128]{2,1,0:T(8,128)} %diss_h.1, bf16[4,48,48,128]{3,2,1,0:T(8,128)(2,1)} %inv_h.1, ...), custom_call_target="tpu_custom_call" | custom-call | tf_op jit(solution)/shard_map/line_relaxation/pallas_call | solution.py:394
  71.7 1.5 %copy.10 = f32[4,48,128]{2,1,0:T(8,128)} copy(f32[4,48,128]{2,1,0:T(8,128)} %line_relaxation.1) | data formatting | bytes 196608
